TPU v7x, 32 devices: a whole 2x2x4 slice. The times are simulated.
32 devices in a mesh: dp: 4 (over y, core), cent: 8 (over z, x).
Axes of the slice: x: 2, y: 2, z: 4, core: 2. Of those that a mesh axis runs over, the one named last changes fastest.
Arguments:
- features: bfloat16 [4096, 1024], P('dp', 'cent'), may hold values from -128 to 128
- centroids: bfloat16 [16384, 1024], P('cent'), may hold values from -2 to 2
- row_weight: float32 [4096], P('dp'), may hold values from 0.5 to 18
- centroid_share: float32 [16384], P('cent'), may hold values from 0.5 to 18
Outputs:
- centroid_means: float32 [1024, 16384], P('dp', 'cent')
- centroid_mass: float32 [16384], P('cent')
All inputs are finite; a program needn't handle non-finite values.
Results may differ from a plain program's by a relative error of at most 0.001.
The roundings to bfloat16 on the way count: a program that leaves them out, or rounds other values in their place, can miss the bound.
Values may be sent and summed in bfloat16 or wider, within the bound.
A program may use at most 64 MiB of HBM per device.

v0:
```python
import jax
import jax.numpy as jnp
from jax import lax
from jax.sharding import PartitionSpec as P

ITERS = 3


def scaled_rows(kernel, column_scale, row_weight):
    row_terms = jnp.sum(kernel * column_scale[None, :], axis=1)
    return row_weight / lax.psum(row_terms, "cent")


def scaled_columns(kernel, row_scale, centroid_share):
    column_terms = jnp.sum(kernel * row_scale[:, None], axis=0)
    return centroid_share / lax.psum(column_terms, "dp")


def per_device(features, centroids, row_weight, centroid_share):
    features_all = lax.all_gather(features, "cent", axis=1, tiled=True)
    scores = lax.dot_general(
        features_all, centroids, (((1,), (1,)), ((), ())), preferred_element_type=jnp.float32
    )
    shared_peak = lax.pmax(jnp.max(scores, axis=1), "cent")
    kernel = jnp.exp(scores - shared_peak[:, None])
    row_scale = scaled_rows(kernel, jnp.ones((kernel.shape[1],), jnp.float32), row_weight)
    column_scale = scaled_columns(kernel, row_scale, centroid_share)
    for iteration in range(ITERS - 1):
        row_scale = scaled_rows(kernel, column_scale, row_weight)
        column_scale = scaled_columns(kernel, row_scale, centroid_share)
    row_scale = scaled_rows(kernel, column_scale, row_weight)
    transport = kernel * row_scale[:, None] * column_scale[None, :]
    centroid_total = lax.psum(jnp.sum(transport, axis=0), "dp")
    weights = transport.astype(jnp.bfloat16)
    weighted = lax.psum_scatter(
        lax.dot_general(
            features_all, weights, (((0,), (0,)), ((), ())), preferred_element_type=jnp.float32
        ),
        "dp",
        scatter_dimension=0,
        tiled=True,
    )
    return (weighted / centroid_total[None, :], centroid_total)


def solution(mesh):
    in_specs = (P("dp", "cent"), P("cent", None), P("dp"), P("cent"))
    out_specs = (P("dp", "cent"), P("cent"))
    return jax.shard_map(
        per_device, mesh=mesh, in_specs=in_specs, out_specs=out_specs, check_vma=False
    )
```

profile of v0, /device:TPU:0, one launch (start us, length us, event | category | flops | bytes accessed | tf_op | source)
XLA Modules:
  0.0 305.7 jit_solution(11417679194362573677)
XLA Ops:
  7.2 0.0 all-gather.2.cloned.1.call-start
  7.2 0.7 all-gather.2.cloned.1.call-update
  7.9 0.0 reduce-scatter.2.cloned.1.call-start
  7.9 55.9 %all-gather.2.cloned.1.call-done = bf16[1024,1024]{1,0:T(8,128)(2,1)} async-done(((bf16[1024,128]{1,0:T(8,128)(2,1)}), bf16[1024,1024]{1,0:T(8,128)(2,1)}) %all-gather.2.cloned.1.call-update) | async-done | bytes 2097168 | tf_op jit(solution)/shard_map/all_gather | solution.py:20
  63.8 10.6 %fusion.6 = (f32[1024]{0:T(1024)S(1)}, f32[1024,2048]{1,0:T(8,128)}) fusion(bf16[1024,1024]{1,0:T(8,128)(2,1)} %all-gather.2.cloned.1.call-done, bf16[2048,1024]{1,0:T(8,128)(2,1)} %param.5), kind=kOutput, calls=%fused_computation.15 | convolution fusion | flops 4297063424 | bytes 14684160 | tf_op jit(solution)/shard_map/dot_general | solution.py:21
  74.4 18.7 %pmax.7 = f32[1024]{0:T(1024)S(1)} all-reduce(f32[1024]{0:T(1024)S(1)} %get-tuple-element.4), channel_id=1, replica_groups=mesh['dp'=4,'cent'=8] {'cent'}, use_global_device_ids=true, to_apply=%region_1.0 | all-reduce | flops 1024 | bytes 8192 | tf_op jit(solution)/shard_map/pmax | solution.py:24
  93.1 4.6 %fusion.5 = f32[1024]{0:T(1024)S(1)} fusion(f32[1024,2048]{1,0:T(8,128)} %get-tuple-element.5, f32[1024]{0:T(1024)S(1)} %pmax.7), kind=kLoop, calls=%fused_computation.14 | loop fusion | flops 4193280 | bytes 8396800 | tf_op jit(solution)/shard_map/reduce_sum | solution.py:10
  97.7 17.7 %psum.56 = f32[1024]{0:T(1024)S(1)} all-reduce(f32[1024]{0:T(1024)S(1)} %fusion.5), channel_id=1, replica_groups=mesh['dp'=4,'cent'=8] {'cent'}, use_global_device_ids=true, to_apply=%region_3.0 | all-reduce | flops 1024 | bytes 8192 | tf_op jit(solution)/shard_map/psum | solution.py:11
  115.5 0.0 copy-done.1
  115.5 4.3 %multiply_reduce_fusion.5 = f32[2048]{0:T(1024)S(1)} fusion(f32[1024]{0:T(1024)S(1)} %div.29, f32[1024,2048]{1,0:T(8,128)} %get-tuple-element.5, f32[1024]{0:T(1024)S(1)} %pmax.7), kind=kLoop, calls=%fused_computation.6 | loop fusion | flops 6289408 | bytes 8404992 | tf_op jit(solution)/shard_map/reduce_sum | solution.py:15
  119.8 5.8 %psum.57 = f32[2048]{0:T(1024)S(1)} all-reduce(f32[2048]{0:T(1024)S(1)} %multiply_reduce_fusion.5), channel_id=1, replica_groups=mesh['dp'=4,'cent'=8] {'dp'}, use_global_device_ids=true, to_apply=%region_5.0 | all-reduce | flops 2048 | bytes 16384 | tf_op jit(solution)/shard_map/psum | solution.py:16
  125.5 0.0 copy-done
  125.6 4.4 %multiply_reduce_fusion.4 = f32[1024]{0:T(1024)S(1)} fusion(f32[2048]{0:T(1024)S(1)} %div.30, f32[1024,2048]{1,0:T(8,128)} %get-tuple-element.5, f32[1024]{0:T(1024)S(1)} %pmax.7), kind=kLoop, calls=%fused_computation.5 | loop fusion | flops 6290432 | bytes 8404992 | tf_op jit(solution)/shard_map/reduce_sum | solution.py:10
  129.9 18.6 %psum.58 = f32[1024]{0:T(1024)S(1)} all-reduce(f32[1024]{0:T(1024)S(1)} %multiply_reduce_fusion.4), channel_id=1, replica_groups=mesh['dp'=4,'cent'=8] {'cent'}, use_global_device_ids=true, to_apply=%region_7.0 | all-reduce | flops 1024 | bytes 8192 | tf_op jit(solution)/shard_map/psum | solution.py:11
  148.5 4.3 %multiply_reduce_fusion.3 = f32[2048]{0:T(1024)S(1)} fusion(f32[1024]{0:T(1024)S(1)} %div.31, f32[1024,2048]{1,0:T(8,128)} %get-tuple-element.5, f32[1024]{0:T(1024)S(1)} %pmax.7), kind=kLoop, calls=%fused_computation.4 | loop fusion | flops 6289408 | bytes 8404992 | tf_op jit(solution)/shard_map/reduce_sum | solution.py:15
  152.8 5.8 %psum.59 = f32[2048]{0:T(1024)S(1)} all-reduce(f32[2048]{0:T(1024)S(1)} %multiply_reduce_fusion.3), channel_id=1, replica_groups=mesh['dp'=4,'cent'=8] {'dp'}, use_global_device_ids=true, to_apply=%region_9.0 | all-reduce | flops 2048 | bytes 16384 | tf_op jit(solution)/shard_map/psum | solution.py:16
  158.6 4.4 %multiply_reduce_fusion.2 = f32[1024]{0:T(1024)S(1)} fusion(f32[2048]{0:T(1024)S(1)} %div.32, f32[1024,2048]{1,0:T(8,128)} %get-tuple-element.5, f32[1024]{0:T(1024)S(1)} %pmax.7), kind=kLoop, calls=%fused_computation.3 | loop fusion | flops 6290432 | bytes 8404992 | tf_op jit(solution)/shard_map/reduce_sum | solution.py:10
  163.0 17.7 %psum.60 = f32[1024]{0:T(1024)S(1)} all-reduce(f32[1024]{0:T(1024)S(1)} %multiply_reduce_fusion.2), channel_id=1, replica_groups=mesh['dp'=4,'cent'=8] {'cent'}, use_global_device_ids=true, to_apply=%region_11.0 | all-reduce | flops 1024 | bytes 8192 | tf_op jit(solution)/shard_map/psum | solution.py:11
  180.7 4.4 %multiply_reduce_fusion.1 = f32[2048]{0:T(1024)S(1)} fusion(f32[1024]{0:T(1024)S(1)} %div.33, f32[1024,2048]{1,0:T(8,128)} %get-tuple-element.5, f32[1024]{0:T(1024)S(1)} %pmax.7), kind=kLoop, calls=%fused_computation.2 | loop fusion | flops 6289408 | bytes 8404992 | tf_op jit(solution)/shard_map/reduce_sum | solution.py:15
  185.1 5.8 %psum.61 = f32[2048]{0:T(1024)S(1)} all-reduce(f32[2048]{0:T(1024)S(1)} %multiply_reduce_fusion.1), channel_id=1, replica_groups=mesh['dp'=4,'cent'=8] {'dp'}, use_global_device_ids=true, to_apply=%region_13.0 | all-reduce | flops 2048 | bytes 16384 | tf_op jit(solution)/shard_map/psum | solution.py:16
  190.9 4.4 %multiply_reduce_fusion = f32[1024]{0:T(1024)S(1)} fusion(f32[2048]{0:T(1024)S(1)} %div.34, f32[1024,2048]{1,0:T(8,128)} %get-tuple-element.5, f32[1024]{0:T(1024)S(1)} %pmax.7), kind=kLoop, calls=%fused_computation.1 | loop fusion | flops 6290432 | bytes 8404992 | tf_op jit(solution)/shard_map/reduce_sum | solution.py:10
  195.3 18.7 %psum.62 = f32[1024]{0:T(1024)S(1)} all-reduce(f32[1024]{0:T(1024)S(1)} %multiply_reduce_fusion), channel_id=1, replica_groups=mesh['dp'=4,'cent'=8] {'cent'}, use_global_device_ids=true, to_apply=%region_15.0 | all-reduce | flops 1024 | bytes 8192 | tf_op jit(solution)/shard_map/psum | solution.py:11
  214.0 0.0 copy-done.3
  214.0 11.3 %convolution_bitcast_fusion = f32[1024,2048]{0,1:T(8,128)} fusion(bf16[1024,1024]{1,0:T(8,128)(2,1)S(1)} %copy-done.3, f32[1024]{0:T(1024)S(1)} %div.35, f32[2048]{0:T(1024)S(1)} %div.34, f32[1024,2048]{1,0:T(8,128)} %get-tuple-element.5, f32[1024]{0:T(1024)S(1)} %pmax.7), kind=kOutput, calls=%fused_computation.10 | convolution fusion | flops 4303355904 | bytes 18890752 | tf_op jit(solution)/shard_map/dot_general | solution.py:36
  225.4 0.0 reduce-scatter.2.cloned.1.call-update
  225.4 4.6 %fusion = f32[2048]{0:T(1024)S(1)} fusion(f32[1024]{0:T(1024)S(1)} %div.35, f32[2048]{0:T(1024)S(1)} %div.34, f32[1024,2048]{1,0:T(8,128)} %get-tuple-element.5, f32[1024]{0:T(1024)S(1)} %pmax.7), kind=kLoop, calls=%fused_computation.8 | loop fusion | flops 8386560 | bytes 8413184 | tf_op jit(solution)/shard_map/reduce_sum | solution.py:33
  230.0 5.8 %psum.63 = f32[2048]{0:T(1024)S(1)} all-reduce(f32[2048]{0:T(1024)S(1)} %fusion), channel_id=1, replica_groups=mesh['dp'=4,'cent'=8] {'dp'}, use_global_device_ids=true, to_apply=%region_18.0 | all-reduce | flops 2048 | bytes 16384 | tf_op jit(solution)/shard_map/psum | solution.py:33
  235.8 0.0 copy-start.2
  235.8 59.2 %reduce-scatter.2.cloned.1.call-done = f32[256,2048]{0,1:T(8,128)} async-done(((f32[1024,2048]{0,1:T(8,128)}), f32[256,2048]{0,1:T(8,128)}) %reduce-scatter.2.cloned.1.call-update) | async-done | bytes 2097168 | tf_op jit(solution)/shard_map/reduce_scatter | solution.py:35
  295.1 1.9 broadcast_divide_fusion
  297.0 1.8 copy.6
  298.8 0.0 copy-done.2
  (10 shorter events, 0.0 us)
Async XLA Ops:
  7.2 56.7 %all-gather.2.cloned.1.call-start = ((), (), s32[]{:S(2)}) async-start(), calls=%async_computation.1 | async-start | bytes 2359296 | tf_op jit(solution)/shard_map/all_gather | solution.py:20
  7.9 287.2 %reduce-scatter.2.cloned.1.call-start = ((), (), s32[]{:S(2)}) async-start(), calls=%async_computation.2 | async-start | bytes 10485760 | tf_op jit(solution)/shard_map/reduce_scatter | solution.py:35
  74.4 41.0 %copy-start.1 = (f32[1024]{0:T(1024)S(1)}, f32[1024]{0:T(1024)}, u32[]{:S(2)}) copy-start(f32[1024]{0:T(1024)} %param.6) | copy-start | bytes 12292
  93.1 32.4 %copy-start = (f32[2048]{0:T(1024)S(1)}, f32[2048]{0:T(1024)}, u32[]{:S(2)}) copy-start(f32[2048]{0:T(1024)} %param.7) | copy-start | bytes 24580
  180.7 33.3 %copy-start.3 = (bf16[1024,1024]{1,0:T(8,128)(2,1)S(1)}, bf16[1024,1024]{1,0:T(8,128)(2,1)}, u32[]{:S(2)}) copy-start(bf16[1024,1024]{1,0:T(8,128)(2,1)} %all-gather.2.cloned.1.call-done) | copy-start | bytes 6291460
  235.8 63.0 %copy-start.2 = (f32[2048]{0:T(1024)}, f32[2048]{0:T(1024)S(1)}, u32[]{:S(2)}) copy-start(f32[2048]{0:T(1024)S(1)} %psum.63) | copy-start | bytes 24580
Sparse Core Ops, SparseCore 0:
  10.0 53.7 all-gather.1
  225.5 69.4 reduce-scatter.1
where the time goes:
time: 306 us
  waiting for transfers between devices  116 us (38%)
  blocking collectives  114 us (37%)
  other arithmetic  37.3 us (12%)
  matrix products  21.9 us (7%)
  between operations  14.2 us (5%)
    psum x4, blocking collectives, scaled_rows(): return row_weight / lax.psum(row_terms, 'cent')  72.7 us
    reduce_scatter x1, waiting for transfers between devices, per_device(): lax.psum_scatter(lax.dot_general(features_all, weights, (((0,), (0,)), ((...  59.2 us
    all_gather x1, waiting for transfers between devices, per_device(): features_all = lax.all_gather(features, 'cent', axis=1, tiled=True)  55.9 us
    pmax x1, blocking collectives, per_device(): shared_peak = lax.pmax(jnp.max(scores, axis=1), 'cent')  18.7 us
    reduce_sum x4, other arithmetic, scaled_rows(): row_terms = jnp.sum(kernel * column_scale[None, :], axis=1)  17.7 us
    psum x3, blocking collectives, scaled_columns(): return centroid_share / lax.psum(column_terms, 'dp')  17.3 us
    reduce_sum x3, other arithmetic, scaled_columns(): column_terms = jnp.sum(kernel * row_scale[:, None], axis=0)  13 us
    dot_general x1, matrix products, per_device(): lax.dot_general(features_all, weights, (((0,), (0,)), ((), ())), preferre...  11.3 us
  transfers between devices with their start and end apart: 2, of which 2 were waited for; matrix products, arithmetic and copies ran while one was open for 2% of the time, Pallas kernels for 0%

commit v1 on v0

v1 whole, which is shorter than its diff:
```python
import functools

import jax
import jax.numpy as jnp
from jax import lax
from jax.experimental import pallas as pl
from jax.experimental.pallas import tpu as pltpu
from jax.sharding import PartitionSpec as P

ITERS = 3
LANES = 128
MESH = pl.DeviceIdType.MESH


def kernel_body(
    nc, nd, nx, nq,
    ft_in, cent_ref, rw_ref, share_ref,
    means_ref, mass_ref,
    ft, kt, wt, xs0, xr0, xs, xr, ys, yr, p1, r1, s2, r2,
    f_send, f_recv, x0_send, x0_recv, x_send, x_recv, y_send, y_recv,
    p1_send, p1_recv, s2_send, s2_recv,
):
    nz = nc // nx
    ny = nd // 2
    me = lax.axis_index("cent")
    md = lax.axis_index("dp")
    z, x = me // nx, me % nx
    y, core = md // 2, md % 2
    dloc, rows = ft_in.shape
    kc = cent_ref.shape[0]
    ds = means_ref.shape[0]
    tiles = rows // LANES
    chunks = kc // LANES
    kq = kc // nq

    barrier = pltpu.get_barrier_semaphore()
    for d in range(1, nc):
        pl.semaphore_signal(barrier, inc=1, device_id={"cent": (me + d) % nc}, device_id_type=MESH)
    for d in range(1, nd):
        pl.semaphore_signal(barrier, inc=1, device_id={"dp": (md + d) % nd}, device_id_type=MESH)
    pl.semaphore_wait(barrier, nc + nd - 2)

    pending = []

    def remote(src, dst, send, recv, target):
        copy = pltpu.make_async_remote_copy(
            src_ref=src, dst_ref=dst, send_sem=send, recv_sem=recv,
            device_id=target, device_id_type=MESH,
        )
        copy.start()
        pending.append(copy)
        return copy

    def slab(j):
        return pl.ds(pl.multiple_of(j * dloc, dloc), dloc)

    inbound = {}
    for dx in range(1, nx):
        target = z * nx + (x + dx) % nx
        inbound[dx] = remote(ft_in, ft.at[slab(me)], f_send.at[dx], f_recv.at[dx], {"cent": target})
    for dz in range(1, nz):
        target = ((z + dz) % nz) * nx + x
        k = dz * nx
        inbound[k] = remote(ft_in, ft.at[slab(me)], f_send.at[k], f_recv.at[k], {"cent": target})
    ft[slab(me), :] = ft_in[...]
    order = sorted(range(1, nz), key=lambda d: min(d, nz - d))
    for dz in order:
        inbound[dz * nx].wait_recv()
        block = ((z + nz - dz) % nz) * nx + x
        for dx in range(1, nx):
            k = dz * nx + dx
            target = z * nx + (x + dx) % nx
            inbound[k] = remote(
                ft.at[slab(block)], ft.at[slab(block)], f_send.at[k], f_recv.at[k], {"cent": target}
            )
    for k in range(1, nc):
        if k % nx or k < nx:
            inbound[k].wait_recv()

    def exchange(axis, n, mine, source, buffer, send, recv):
        buffer[pl.ds(mine, 1)] = source[...][None]
        copies = [
            remote(source, buffer.at[mine], send.at[d], recv.at[d], {axis: (mine + d) % n})
            for d in range(1, n)
        ]
        for copy in copies:
            copy.wait_recv()
        return buffer[...]

    def chunk(i):
        return pl.ds(pl.multiple_of(i * LANES, LANES), LANES)

    def lane(t):
        return slice(t * LANES, (t + 1) * LANES)

    def fold(block):
        return jnp.sum(block.reshape(LANES // 8, 8, LANES), axis=0)

    def row_vector(parts):
        return jnp.concatenate([jnp.sum(p, axis=0, keepdims=True) for p in parts], axis=1)

    step = 2 * LANES

    def score(i, peak):
        at = pl.ds(pl.multiple_of(i * step, step), step)
        s = jnp.dot(cent_ref[at, :], ft[...], preferred_element_type=jnp.float32)
        kt[at, :] = s
        return jnp.maximum(peak, jnp.max(s.reshape(step // 8, 8, rows), axis=0))

    peak = lax.fori_loop(0, kc // step, score, jnp.full((8, rows), -jnp.inf, jnp.float32))
    peak = jnp.max(peak, axis=0, keepdims=True)

    zeros = tuple(jnp.zeros((8, LANES), jnp.float32) for t in range(tiles))

    def exponent(i, parts):
        out = []
        for t in range(tiles):
            e = jnp.exp(kt[chunk(i), lane(t)] - peak[:, lane(t)])
            kt[chunk(i), lane(t)] = e
            out.append(parts[t] + fold(e))
        return tuple(out)

    local = row_vector(lax.fori_loop(0, chunks, exponent, zeros))
    xs0[0:1, :] = peak
    xs0[1:2, :] = local
    both = exchange("cent", nc, me, xs0, xr0, x0_send, x0_recv)
    top = jnp.max(both[:, 0, :], axis=0, keepdims=True)
    total = jnp.sum(both[:, 1, :] * jnp.exp(both[:, 0, :] - top), axis=0, keepdims=True)
    shift = jnp.exp(peak - top)
    weight = rw_ref[...]
    row_scale = weight / total * shift

    def columns(row_scale, k):
        def one(i, carry):
            acc = kt[chunk(i), lane(0)] * row_scale[:, lane(0)]
            for t in range(1, tiles):
                acc = acc + kt[chunk(i), lane(t)] * row_scale[:, lane(t)]
            ys[k, :, chunk(i)] = jnp.sum(acc.T, axis=0, keepdims=True)
            return carry

        lax.fori_loop(0, chunks, one, 0)
        sums = exchange("dp", nd, md, ys.at[k], yr.at[k], y_send.at[k], y_recv.at[k])
        return jnp.sum(sums, axis=0)

    def down(ref, i):
        return jnp.broadcast_to(ref[:, chunk(i)], (LANES, LANES)).T

    for k in range(ITERS):
        mass_ref[...] = share_ref[...] / columns(row_scale, k)

        def one(i, parts):
            scale = down(mass_ref, i)
            return tuple(parts[t] + fold(kt[chunk(i), lane(t)] * scale) for t in range(tiles))

        xs[k] = row_vector(lax.fori_loop(0, chunks, one, zeros)) * shift
        sums = exchange("cent", nc, me, xs.at[k], xr.at[k], x_send.at[k], x_recv.at[k])
        row_scale = weight / jnp.sum(sums, axis=0) * shift

    def transport(i, carry):
        scale = down(mass_ref, i)
        acc = jnp.zeros((LANES, LANES), jnp.float32)
        for t in range(tiles):
            v = kt[chunk(i), lane(t)] * row_scale[:, lane(t)] * scale
            wt[chunk(i), lane(t)] = v.astype(jnp.bfloat16)
            acc = acc + v
        ys[ITERS, :, chunk(i)] = jnp.sum(acc.T, axis=0, keepdims=True)
        return carry

    lax.fori_loop(0, chunks, transport, 0)
    yr[ITERS, pl.ds(md, 1)] = ys[ITERS][None]
    mass_copies = [
        remote(
            ys.at[ITERS], yr.at[ITERS, md], y_send.at[ITERS, d], y_recv.at[ITERS, d],
            {"dp": (md + d) % nd},
        )
        for d in range(1, nd)
    ]

    def partial(owner, q):
        at = pl.ds(pl.multiple_of(owner * ds, ds), ds)
        return lax.dot_general(
            ft[at, :], wt[q * kq:(q + 1) * kq, :], (((1,), (1,)), ((), ())),
            preferred_element_type=jnp.float32,
        )

    pair = y * 2 + (1 - core)
    first = {}

    def to_core(dy, q):
        p1[dy, q] = partial(((y + dy) % ny) * 2 + (1 - core), q)
        first[dy, q] = remote(
            p1.at[dy, q], r1.at[dy, q], p1_send.at[dy, q], p1_recv.at[dy, q], {"dp": pair}
        )

    second = {}

    def along_y(dy, q):
        owner = ((y + dy) % ny) * 2 + core
        mine = partial(owner, q)
        first[dy, q].wait_recv()
        s2[dy - 1, q] = mine + r1[dy, q]
        second[dy, q] = remote(
            s2.at[dy - 1, q], r2.at[dy - 1, q],
            s2_send.at[dy - 1, q], s2_recv.at[dy - 1, q], {"dp": owner},
        )

    todo = [(dy, q) for q in range(nq) for dy in range(1, ny)]
    to_core(*todo[0])
    for i, item in enumerate(todo):
        if i + 1 < len(todo):
            to_core(*todo[i + 1])
        along_y(*item)
    for q in range(nq):
        to_core(0, q)
    for copy in mass_copies:
        copy.wait_recv()
    mass = jnp.sum(yr[ITERS], axis=0)
    mass_ref[...] = mass
    for q in range(nq):
        mine = partial(md, q)
        first[0, q].wait_recv()
        means_ref[:, q * kq:(q + 1) * kq] = mine + r1[0, q]
    for q in range(nq):
        at = slice(q * kq, (q + 1) * kq)
        value = means_ref[:, at]
        for dy in range(1, ny):
            second[dy, q].wait_recv()
            value = value + r2[dy - 1, q]
        means_ref[:, at] = value / mass[:, at]

    for copy in pending:
        copy.wait_send()


def solution(mesh):
    nc, nd = mesh.shape["cent"], mesh.shape["dp"]
    ny = nd // 2
    nx = ny if nc % ny == 0 else 1
    nq = 8

    def per_device(features, centroids, row_weight, centroid_share):
        rows, dloc = features.shape
        kc, width = centroids.shape
        ds = width // nd
        f32, bf16 = jnp.float32, jnp.bfloat16
        dma = pltpu.SemaphoreType.DMA
        vmem = pl.BlockSpec(memory_space=pltpu.VMEM)
        means, mass = pl.pallas_call(
            functools.partial(kernel_body, nc, nd, nx, nq),
            out_shape=(
                jax.ShapeDtypeStruct((ds, kc), f32),
                jax.ShapeDtypeStruct((1, kc), f32),
            ),
            in_specs=[vmem] * 4,
            out_specs=(vmem, vmem),
            scratch_shapes=[
                pltpu.VMEM((width, rows), bf16),
                pltpu.VMEM((kc, rows), f32),
                pltpu.VMEM((kc, rows), bf16),
                pltpu.VMEM((2, rows), f32),
                pltpu.VMEM((nc, 2, rows), f32),
                pltpu.VMEM((ITERS, 1, rows), f32),
                pltpu.VMEM((ITERS, nc, 1, rows), f32),
                pltpu.VMEM((ITERS + 1, 1, kc), f32),
                pltpu.VMEM((ITERS + 1, nd, 1, kc), f32),
                pltpu.VMEM((ny, nq, ds, kc // nq), f32),
                pltpu.VMEM((ny, nq, ds, kc // nq), f32),
                pltpu.VMEM((ny - 1, nq, ds, kc // nq), f32),
                pltpu.VMEM((ny - 1, nq, ds, kc // nq), f32),
                dma((nc,)), dma((nc,)),
                dma((nc,)), dma((nc,)),
                dma((ITERS, nc)), dma((ITERS, nc)),
                dma((ITERS + 1, nd)), dma((ITERS + 1, nd)),
                dma((ny, nq)), dma((ny, nq)),
                dma((ny - 1, nq)), dma((ny - 1, nq)),
            ],
            compiler_params=pltpu.CompilerParams(
                collective_id=0, has_side_effects=True, vmem_limit_bytes=50 * 1024 * 1024
            ),
        )(features.T, centroids, row_weight[None], centroid_share[None])
        return means, mass[0]

    in_specs = (P("dp", "cent"), P("cent", None), P("dp"), P("cent"))
    out_specs = (P("dp", "cent"), P("cent"))
    return jax.shard_map(
        per_device, mesh=mesh, in_specs=in_specs, out_specs=out_specs, check_vma=False
    )
```

time: 306 us -> 145 us (0.47)
  Pallas kernels: 0 us -> 139 us
  waiting for transfers between devices: 116 us -> 0 us
  blocking collectives: 114 us -> 0 us
  other arithmetic: 37.3 us -> 0 us
  matrix products: 21.9 us -> 0 us
  between operations: 14.2 us -> 0.65 us
    pallas_call x0 -> x1, Pallas kernels: none -> 139 us  [per_device(): pl.pallas_call(functools.partial(kernel_body, nc, nd, nx, nq), out_shape=...]
    psum x8 -> x0, blocking collectives: 95.8 us -> none  [the longest x4 72.7 us: scaled_rows(): return row_weight / lax.psum(row_terms, 'cent')]
    reduce_scatter x1 -> x0, waiting for transfers between devices: 59.2 us -> none  [per_device(): lax.psum_scatter(lax.dot_general(features_all, weights, (((0,), (0,)), ((...]
    all_gather x1 -> x0, waiting for transfers between devices: 55.9 us -> none  [per_device(): features_all = lax.all_gather(features, 'cent', axis=1, tiled=True)]
    reduce_sum x8 -> x0, other arithmetic: 35.3 us -> none  [the longest x4 17.7 us: scaled_rows(): row_terms = jnp.sum(kernel * column_scale[None, :], axis=1)]
    dot_general x2 -> x0, matrix products: 21.9 us -> none  [the longest x1 11.3 us: per_device(): lax.dot_general(features_all, weights, (((0,), (0,)), ((), ())), preferre...]
    pmax x1 -> x0, blocking collectives: 18.7 us -> none  [per_device(): shared_peak = lax.pmax(jnp.max(scores, axis=1), 'cent')]
  transfers between devices with their start and end apart: 2 -> 0, of which waited for: 2 -> 0; matrix products, arithmetic and copies ran while one was open for 2% -> 0% of each run, Pallas kernels for 0% -> 0%
where the time goes in v1:
time: 145 us; the launch traced here: 144 us
  Pallas kernels  139 us (96%)
  local copies, waits for them, and re-layouts  4.38 us (3%)
    pallas_call x1, Pallas kernels, per_device(): pl.pallas_call(functools.partial(kernel_body, nc, nd, nx, nq), out_shape=...  139 us
    unnamed x7, local copies, waits for them, and re-layouts  4.38 us

profile of v1, /device:TPU:0, one launch (start us, length us, event | category | flops | bytes accessed | tf_op | source)
XLA Modules:
  0.0 144.5 jit_solution(11099584937307866535)
XLA Ops:
  0.6 1.1 copy.6
  1.7 0.0 copy-start
  1.7 0.7 copy-done
  2.4 0.0 copy-start.1
  2.4 0.7 copy-done.1
  3.1 139.5 %shard_map.59 = (f32[256,2048]{1,0:T(8,128)S(1)}, f32[1,2048]{1,0:T(1,128)S(1)}) custom-call(bf16[128,1024]{1,0:T(8,128)(2,1)S(1)} %bitcast.4, bf16[2048,1024]{1,0:T(8,128)(2,1)} %cent_ref.1, f32[1,1024]{1,0:T(1,128)S(1)} %bitcast.7, f32[1,2048]{1,0:T(1,128)S(1)} %bitcast.5), custom_call_target="tpu_custom_call" | custom-call | tf_op jit(solution)/shard_map/pallas_call | solution.py:248
  142.6 1.3 copy.9
  143.9 0.6 copy.10
Async XLA Ops:
  1.7 0.7 copy-start
  2.4 0.7 copy-start.1

commit v2 on v1

--- a/solution.py
+++ b/solution.py
@@ -16,7 +16,7 @@
     nc, nd, nx, nq,
     ft_in, cent_ref, rw_ref, share_ref,
     means_ref, mass_ref,
-    ft, kt, wt, xs0, xr0, xs, xr, ys, yr, p1, r1, s2, r2,
+    cent, load_sem, ft, kt, wt, xs0, xr0, xs, xr, ys, yr, p1, r1, s2, r2,
     f_send, f_recv, x0_send, x0_recv, x_send, x_recv, y_send, y_recv,
     p1_send, p1_recv, s2_send, s2_recv,
 ):
@@ -54,28 +54,43 @@
     def slab(j):
         return pl.ds(pl.multiple_of(j * dloc, dloc), dloc)
 
+    load = pltpu.make_async_copy(cent_ref, cent, load_sem)
+    load.start()
+
+    half = dloc // 2
     inbound = {}
-    for dx in range(1, nx):
-        target = z * nx + (x + dx) % nx
-        inbound[dx] = remote(ft_in, ft.at[slab(me)], f_send.at[dx], f_recv.at[dx], {"cent": target})
-    for dz in range(1, nz):
-        target = ((z + dz) % nz) * nx + x
-        k = dz * nx
-        inbound[k] = remote(ft_in, ft.at[slab(me)], f_send.at[k], f_recv.at[k], {"cent": target})
+
+    def send(source, block, k, piece, target):
+        at = pl.ds(pl.multiple_of(block * dloc + piece * half, half), half)
+        inbound[k, piece] = remote(
+            ft.at[at] if source is None else source.at[piece * half:(piece + 1) * half],
+            ft.at[at], f_send.at[k, piece], f_recv.at[k, piece], {"cent": target},
+        )
+
+    up = ((z + 1) % nz) * nx + x
+    low = ((z + nz - 1) % nz) * nx + x
+    ups, downs = nz // 2, (nz - 1) // 2
+    for piece in range(2):
+        if ups:
+            send(ft_in, me, nx, piece, up)
+        if downs:
+            send(ft_in, me, (nz - 1) * nx, piece, low)
+        for dx in range(1, nx):
+            send(ft_in, me, dx, piece, z * nx + (x + dx) % nx)
     ft[slab(me), :] = ft_in[...]
-    order = sorted(range(1, nz), key=lambda d: min(d, nz - d))
-    for dz in order:
-        inbound[dz * nx].wait_recv()
-        block = ((z + nz - dz) % nz) * nx + x
-        for dx in range(1, nx):
-            k = dz * nx + dx
-            target = z * nx + (x + dx) % nx
-            inbound[k] = remote(
-                ft.at[slab(block)], ft.at[slab(block)], f_send.at[k], f_recv.at[k], {"cent": target}
-            )
-    for k in range(1, nc):
-        if k % nx or k < nx:
-            inbound[k].wait_recv()
+    seen = [0]
+    for hop in range(1, ups + 1):
+        here = [(hop, up, ups)] + ([(nz - hop, low, downs)] if hop <= downs else [])
+        for piece in range(2):
+            for dz, onward, most in here:
+                inbound[dz * nx, piece].wait_recv()
+                block = ((z + nz - dz) % nz) * nx + x
+                if hop < most:
+                    ahead = dz + 1 if onward is up else dz - 1
+                    send(None, block, ahead * nx, piece, onward)
+                for dx in range(1, nx):
+                    send(None, block, dz * nx + dx, piece, z * nx + (x + dx) % nx)
+        seen += [dz for dz, onward, most in here]
 
     def exchange(axis, n, mine, source, buffer, send, recv):
         buffer[pl.ds(mine, 1)] = source[...][None]
@@ -99,15 +114,27 @@
     def row_vector(parts):
         return jnp.concatenate([jnp.sum(p, axis=0, keepdims=True) for p in parts], axis=1)
 
+    load.wait()
     step = 2 * LANES
-
-    def score(i, peak):
-        at = pl.ds(pl.multiple_of(i * step, step), step)
-        s = jnp.dot(cent_ref[at, :], ft[...], preferred_element_type=jnp.float32)
-        kt[at, :] = s
-        return jnp.maximum(peak, jnp.max(s.reshape(step // 8, 8, rows), axis=0))
-
-    peak = lax.fori_loop(0, kc // step, score, jnp.full((8, rows), -jnp.inf, jnp.float32))
+    group = nx * dloc
+    peak = jnp.full((8, rows), -jnp.inf, jnp.float32)
+    for n, dz in enumerate(seen):
+        for dx in range(1, nx):
+            for piece in range(2):
+                inbound[dz * nx + dx, piece].wait_recv()
+        across = pl.ds(pl.multiple_of(((z + nz - dz) % nz) * group, group), group)
+
+        def score(i, peak, n=n, across=across):
+            at = pl.ds(pl.multiple_of(i * step, step), step)
+            s = jnp.dot(cent[at, across], ft[across, :], preferred_element_type=jnp.float32)
+            if n:
+                s = s + kt[at, :]
+            kt[at, :] = s
+            if n < nz - 1:
+                return peak
+            return jnp.maximum(peak, jnp.max(s.reshape(step // 8, 8, rows), axis=0))
+
+        peak = lax.fori_loop(0, kc // step, score, peak)
     peak = jnp.max(peak, axis=0, keepdims=True)
 
     zeros = tuple(jnp.zeros((8, LANES), jnp.float32) for t in range(tiles))
@@ -251,9 +278,11 @@
                 jax.ShapeDtypeStruct((ds, kc), f32),
                 jax.ShapeDtypeStruct((1, kc), f32),
             ),
-            in_specs=[vmem] * 4,
+            in_specs=[vmem, pl.BlockSpec(memory_space=pl.ANY), vmem, vmem],
             out_specs=(vmem, vmem),
             scratch_shapes=[
+                pltpu.VMEM((kc, width), bf16),
+                dma(()),
                 pltpu.VMEM((width, rows), bf16),
                 pltpu.VMEM((kc, rows), f32),
                 pltpu.VMEM((kc, rows), bf16),
@@ -267,7 +296,7 @@
                 pltpu.VMEM((ny, nq, ds, kc // nq), f32),
                 pltpu.VMEM((ny - 1, nq, ds, kc // nq), f32),
                 pltpu.VMEM((ny - 1, nq, ds, kc // nq), f32),
-                dma((nc,)), dma((nc,)),
+                dma((nc, 2)), dma((nc, 2)),
                 dma((nc,)), dma((nc,)),
                 dma((ITERS, nc)), dma((ITERS, nc)),
                 dma((ITERS + 1, nd)), dma((ITERS + 1, nd)),

time: 145 us -> 130 us (0.90)
  Pallas kernels: 139 us -> 125 us
    pallas_call x1, Pallas kernels: 139 us -> 125 us  [per_device(): pl.pallas_call(functools.partial(kernel_body, nc, nd, nx, nq), out_shape=...]
where the time goes in v2:
time: 130 us
  Pallas kernels  125 us (96%)
  local copies, waits for them, and re-layouts  4.38 us (3%)
    pallas_call x1, Pallas kernels, per_device(): pl.pallas_call(functools.partial(kernel_body, nc, nd, nx, nq), out_shape=...  125 us
    unnamed x7, local copies, waits for them, and re-layouts  4.38 us

profile of v2, /device:TPU:0, one launch (start us, length us, event | category | flops | bytes accessed | tf_op | source)
XLA Modules:
  0.0 129.7 jit_solution(16617205849575541219)
XLA Ops:
  0.6 1.1 copy.6
  1.7 0.0 copy-start
  1.7 0.7 copy-done
  2.4 0.0 copy-start.1
  2.4 0.7 copy-done.1
  3.1 124.7 %shard_map.59 = (f32[256,2048]{1,0:T(8,128)S(1)}, f32[1,2048]{1,0:T(1,128)S(1)}) custom-call(bf16[128,1024]{1,0:T(8,128)(2,1)S(1)} %bitcast.4, bf16[2048,1024]{1,0:T(8,128)(2,1)} %cent_ref.1, f32[1,1024]{1,0:T(1,128)S(1)} %bitcast.7, f32[1,2048]{1,0:T(1,128)S(1)} %bitcast.5), custom_call_target="tpu_custom_call" | custom-call | tf_op jit(solution)/shard_map/pallas_call | solution.py:275
  127.8 1.3 %copy.9 = f32[256,2048]{1,0:T(8,128)} copy(f32[256,2048]{1,0:T(8,128)S(1)} %get-tuple-element.8) | data formatting | bytes 4194304
  129.1 0.6 copy.10
Async XLA Ops:
  1.7 0.7 copy-start
  2.4 0.7 copy-start.1

commit v3 on v2

--- a/solution.py
+++ b/solution.py
@@ -16,7 +16,7 @@
     nc, nd, nx, nq,
     ft_in, cent_ref, rw_ref, share_ref,
     means_ref, mass_ref,
-    cent, load_sem, ft, kt, wt, xs0, xr0, xs, xr, ys, yr, p1, r1, s2, r2,
+    cent, load_sem, ft, kt, wt, xs0, xr0, xs, xr, ys, yr, p1, r1, s2, r2, s2n, r2n,
     f_send, f_recv, x0_send, x0_recv, x_send, x_recv, y_send, y_recv,
     p1_send, p1_recv, s2_send, s2_recv,
 ):
@@ -220,14 +220,23 @@
         )
 
     second = {}
+    wide = s2.shape[1]
+
+    def outgoing(q):
+        return (s2, q) if q < wide else (s2n, q - wide)
+
+    def incoming(q):
+        return (r2, q) if q < wide else (r2n, q - wide)
 
     def along_y(dy, q):
         owner = ((y + dy) % ny) * 2 + core
         mine = partial(owner, q)
         first[dy, q].wait_recv()
-        s2[dy - 1, q] = mine + r1[dy, q]
+        out, slot = outgoing(q)
+        out[dy - 1, slot] = (mine + r1[dy, q]).astype(out.dtype)
+        arriving, slot = incoming(q)
         second[dy, q] = remote(
-            s2.at[dy - 1, q], r2.at[dy - 1, q],
+            out.at[dy - 1, slot], arriving.at[dy - 1, slot],
             s2_send.at[dy - 1, q], s2_recv.at[dy - 1, q], {"dp": owner},
         )
 
@@ -252,7 +261,8 @@
         value = means_ref[:, at]
         for dy in range(1, ny):
             second[dy, q].wait_recv()
-            value = value + r2[dy - 1, q]
+            arrived, slot = incoming(q)
+            value = value + arrived[dy - 1, slot].astype(jnp.float32)
         means_ref[:, at] = value / mass[:, at]
 
     for copy in pending:
@@ -264,6 +274,7 @@
     ny = nd // 2
     nx = ny if nc % ny == 0 else 1
     nq = 8
+    narrow = nq // 4
 
     def per_device(features, centroids, row_weight, centroid_share):
         rows, dloc = features.shape
@@ -294,8 +305,10 @@
                 pltpu.VMEM((ITERS + 1, nd, 1, kc), f32),
                 pltpu.VMEM((ny, nq, ds, kc // nq), f32),
                 pltpu.VMEM((ny, nq, ds, kc // nq), f32),
-                pltpu.VMEM((ny - 1, nq, ds, kc // nq), f32),
-                pltpu.VMEM((ny - 1, nq, ds, kc // nq), f32),
+                pltpu.VMEM((ny - 1, nq - narrow, ds, kc // nq), f32),
+                pltpu.VMEM((ny - 1, nq - narrow, ds, kc // nq), f32),
+                pltpu.VMEM((ny - 1, narrow, ds, kc // nq), bf16),
+                pltpu.VMEM((ny - 1, narrow, ds, kc // nq), bf16),
                 dma((nc, 2)), dma((nc, 2)),
                 dma((nc,)), dma((nc,)),
                 dma((ITERS, nc)), dma((ITERS, nc)),

time: 130 us -> 124 us (0.954)
  Pallas kernels: 125 us -> 119 us
    pallas_call x1, Pallas kernels: 125 us -> 119 us  [per_device(): pl.pallas_call(functools.partial(kernel_body, nc, nd, nx, nq), out_shape=...]
where the time goes in v3:
time: 124 us
  Pallas kernels  119 us (96%)
  local copies, waits for them, and re-layouts  4.38 us (4%)
    pallas_call x1, Pallas kernels, per_device(): pl.pallas_call(functools.partial(kernel_body, nc, nd, nx, nq), out_shape=...  119 us
    unnamed x7, local copies, waits for them, and re-layouts  4.38 us

profile of v3, /device:TPU:0, one launch (start us, length us, event | category | flops | bytes accessed | tf_op | source)
XLA Modules:
  0.0 124.1 jit_solution(8666923894499286411)
XLA Ops:
  0.6 1.1 copy.6
  1.7 0.0 copy-start
  1.7 0.7 copy-done
  2.4 0.0 copy-start.1
  2.4 0.7 copy-done.1
  3.1 119.0 %shard_map.59 = (f32[256,2048]{1,0:T(8,128)S(1)}, f32[1,2048]{1,0:T(1,128)S(1)}) custom-call(bf16[128,1024]{1,0:T(8,128)(2,1)S(1)} %bitcast.4, bf16[2048,1024]{1,0:T(8,128)(2,1)} %cent_ref.1, f32[1,1024]{1,0:T(1,128)S(1)} %bitcast.7, f32[1,2048]{1,0:T(1,128)S(1)} %bitcast.5), custom_call_target="tpu_custom_call" | custom-call | tf_op jit(solution)/shard_map/pallas_call | solution.py:286
  122.2 1.3 %copy.9 = f32[256,2048]{1,0:T(8,128)} copy(f32[256,2048]{1,0:T(8,128)S(1)} %get-tuple-element.8) | data formatting | bytes 4194304
  123.5 0.6 copy.10
Async XLA Ops:
  1.7 0.7 copy-start
  2.4 0.7 copy-start.1
